TPU v7x, 32 devices: a whole 2x2x4 slice. The times are simulated.
32 devices in a mesh: dp: 4 (over x, core), fsdp: 8 (over z, y).
Axes of the slice: x: 2, y: 2, z: 4, core: 2. Of those that a mesh axis runs over, the one named last changes fastest.
Arguments:
- query_in: bfloat16 [7168, 1024], P(('dp', 'fsdp')), may hold values from -32 to 32
- key_in: bfloat16 [7168, 1024], P(('dp', 'fsdp')), may hold values from -32 to 32
- value_in: bfloat16 [7168, 1024], P(('dp', 'fsdp')), may hold values from -6 to 6
- length_plan: int32 [32, 224], P(('dp', 'fsdp')), may hold values from 0 to 223, each once within a row
- segment_ids: int32 [32, 224], P(('dp', 'fsdp')), may hold values from 0 to 3, never falling along the last dimension, each value on 1 to 112 neighbouring positions
- out_grad: bfloat16 [7168, 1024], P(('dp', 'fsdp')), may hold values from -6 to 6
- query_gain: float32 [128], replicated, may hold values from 0.7 to 6
- key_gain: float32 [128], replicated, may hold values from 0.7 to 6
Outputs:
- query_grad: bfloat16 [7168, 1024], P(('dp', 'fsdp'))
- key_grad: bfloat16 [7168, 1024], P(('dp', 'fsdp'))
- value_grad: bfloat16 [7168, 1024], P(('dp', 'fsdp'))
- query_gain_grad: float32 [128], replicated
- key_gain_grad: float32 [128], replicated
Inputs may be any that keep to these rules, and one draw needn't show every extreme that they name: `length_plan`: each row is a permutation of 0 to 223. `segment_ids`: within a row the numbers never fall; each utterance piece holds 1 to 112 frames, and one holds exactly 112.
All inputs are finite; a program needn't handle non-finite values.
Results may differ from a plain program's by a relative error of at most 0.01.
The roundings to bfloat16 on the way count: a program that leaves them out, or rounds other values in their place, can miss the bound.
Values may be sent and summed in bfloat16 or wider, within the bound.
A program may use at most 64 MiB of HBM per device.

v0:
```python
import jax
import jax.numpy as jnp
from jax import lax
from jax.sharding import PartitionSpec as P

HEAD = 128


def normalize(raw, gain):
    frames = raw.shape[0]
    values = raw.astype(jnp.float32).reshape(frames, -1, HEAD)
    inv_rms = lax.rsqrt(jnp.mean(values * values, axis=-1, keepdims=True) + 1e-06)
    unit_vec = values * inv_rms
    return (unit_vec, inv_rms, (unit_vec * gain).astype(jnp.bfloat16))


def norm_back(d_norm, unit_vec, inv_rms, gain):
    d_unit = d_norm * gain
    inner = jnp.mean(d_unit * unit_vec, axis=-1, keepdims=True)
    result = inv_rms * (d_unit - unit_vec * inner)
    return result.reshape(result.shape[0], -1).astype(jnp.bfloat16)


def attend_heads(query_pk, key_pk, value_pk, grad_rows, segment_row, query_gain, key_gain):
    frames = query_pk.shape[0]
    score_scale = HEAD ** (-0.5)
    q_unit, q_inv, q_norm = normalize(query_pk, query_gain)
    k_unit, k_inv, k_norm = normalize(key_pk, key_gain)
    scores = (
        jnp.einsum("thd,shd->hts", q_norm, k_norm, preferred_element_type=jnp.float32) * score_scale
    )
    same_seg = segment_row[:, None] == segment_row[None, :]
    scores = jnp.where(same_seg[None], scores, -jnp.inf)
    row_max = jnp.max(scores, axis=-1, keepdims=True)
    exponent = jnp.exp(scores - row_max)
    attn_probs = exponent / jnp.sum(exponent, axis=-1, keepdims=True)
    value_heads = value_pk.reshape(frames, -1, HEAD)
    grad_heads = grad_rows.reshape(frames, -1, HEAD)
    probs_half = attn_probs.astype(jnp.bfloat16)
    output = jnp.einsum("hts,shd->thd", probs_half, value_heads, preferred_element_type=jnp.float32)
    row_delta = jnp.sum(grad_heads.astype(jnp.float32) * output, axis=-1)
    value_grad = jnp.einsum(
        "hts,thd->shd", probs_half, grad_heads, preferred_element_type=jnp.float32
    )
    value_grad = value_grad.astype(jnp.bfloat16).reshape(frames, -1)
    d_prob = jnp.einsum("thd,shd->hts", grad_heads, value_heads, preferred_element_type=jnp.float32)
    d_score = (attn_probs * (d_prob - row_delta.T[:, :, None]) * score_scale).astype(jnp.bfloat16)
    d_qnorm = jnp.einsum("hts,shd->thd", d_score, k_norm, preferred_element_type=jnp.float32)
    d_knorm = jnp.einsum("hts,thd->shd", d_score, q_norm, preferred_element_type=jnp.float32)
    query_part = jnp.sum(d_qnorm * q_unit, axis=(0, 1))
    key_part = jnp.sum(d_knorm * k_unit, axis=(0, 1))
    query_grad = norm_back(d_qnorm, q_unit, q_inv, query_gain)
    key_grad = norm_back(d_knorm, k_unit, k_inv, key_gain)
    return (query_grad, key_grad, value_grad, query_part, key_part)


def on_device(query_in, key_in, value_in, length_plan, segment_ids, out_grad, query_gain, key_gain):
    frames = query_in.shape[0]
    positions = jnp.arange(frames, dtype=jnp.int32)
    inverse = jnp.zeros((frames,), jnp.int32).at[length_plan[0]].set(positions)
    send_query = query_in[inverse]
    send_key = key_in[inverse]
    send_value = value_in[inverse]
    segment_row = segment_ids[0]
    query_pk, key_pk, value_pk = (
        lax.all_to_all(send_query, "dp", split_axis=0, concat_axis=0, tiled=True),
        lax.all_to_all(send_key, "dp", split_axis=0, concat_axis=0, tiled=True),
        lax.all_to_all(send_value, "dp", split_axis=0, concat_axis=0, tiled=True),
    )
    query_grad, key_grad, value_grad, query_part, key_part = attend_heads(
        query_pk, key_pk, value_pk, out_grad, segment_row, query_gain, key_gain
    )
    query_total, key_total = lax.psum((query_part, key_part), ("dp", "fsdp"))
    return (query_grad, key_grad, value_grad, query_total, key_total)


def solution(mesh):
    in_specs = (
        P(("dp", "fsdp"), None),
        P(("dp", "fsdp"), None),
        P(("dp", "fsdp"), None),
        P(("dp", "fsdp"), None),
        P(("dp", "fsdp"), None),
        P(("dp", "fsdp"), None),
        P(),
        P(),
    )
    out_specs = (
        P(("dp", "fsdp"), None),
        P(("dp", "fsdp"), None),
        P(("dp", "fsdp"), None),
        P(),
        P(),
    )
    return jax.shard_map(
        on_device, mesh=mesh, in_specs=in_specs, out_specs=out_specs, check_vma=False
    )
```

profile of v0, /device:TPU:0, one launch (start us, length us, event | category | flops | bytes accessed | tf_op | source)
XLA Modules:
  0.0 95.4 jit_solution(11264698559020234635)
XLA Ops:
  0.6 0.0 copy-start
  0.6 0.7 compare_select_fusion
  1.4 1.3 %scatter_custom_fusion = s32[224]{0:T(256)S(1)} fusion(s32[224]{0:T(256)S(1)} %bitcast.88, s32[224]{0:T(256)S(1)} %iota.3, s32[]{:T(128)} %constant.4.clone.1), kind=kCustom, calls=%fused_computation.55 | custom fusion | bytes 900 | tf_op jit(solution)/shard_map/scatter | solution.py:60
  2.7 0.0 copy-start.1
  2.7 3.3 %gather_fusion.2 = bf16[224,1024]{1,0:T(8,128)(2,1)} fusion(bf16[224,1024]{1,0:T(8,128)(2,1)} %param.10, s32[1024]{0:T(1024)S(1)} %pad_clamp_fusion), kind=kCustom, calls=%fused_computation.2 | custom fusion | bytes 918400 | tf_op jit(solution)/shard_map/gather | solution.py:63
  6.1 4.2 %all-to-all-start.2 = ((bf16[4,56,1024]{2,1,0:T(8,128)(2,1)}), bf16[4,56,1024]{2,1,0:T(8,128)(2,1)S(1)}, u32[]{:S(2)}, u32[]{:S(2)}) async-start(bf16[4,56,1024]{2,1,0:T(8,128)(2,1)} %bitcast.5), calls=%async_computation.2 | async-start | bytes 917504 | tf_op jit(solution)/shard_map/all_to_all | solution.py:68
  10.3 0.0 copy-done.1
  10.3 0.0 copy-start.2
  10.3 1.9 %gather_fusion = bf16[224,1024]{1,0:T(8,128)(2,1)} fusion(bf16[224,1024]{1,0:T(8,128)(2,1)S(1)} %copy-done.1, s32[1024]{0:T(1024)S(1)} %pad_clamp_fusion), kind=kCustom, calls=%fused_computation | custom fusion | bytes 918400 | tf_op jit(solution)/shard_map/gather | solution.py:61
  12.1 6.3 %all-to-all-done.2 = bf16[4,56,1024]{2,1,0:T(8,128)(2,1)S(1)} async-done(((bf16[4,56,1024]{2,1,0:T(8,128)(2,1)}), bf16[4,56,1024]{2,1,0:T(8,128)(2,1)S(1)}, u32[]{:S(2)}, u32[]{:S(2)}) %all-to-all-start.2) | async-done | bytes 458784 | tf_op jit(solution)/shard_map/all_to_all | solution.py:68
  18.4 3.5 %all-to-all-start = ((bf16[4,56,1024]{2,1,0:T(8,128)(2,1)}), bf16[4,56,1024]{2,1,0:T(8,128)(2,1)S(1)}, u32[]{:S(2)}, u32[]{:S(2)}) async-start(bf16[4,56,1024]{2,1,0:T(8,128)(2,1)} %bitcast.2), calls=%async_computation | async-start | bytes 917504 | tf_op jit(solution)/shard_map/all_to_all | solution.py:66
  21.9 0.0 copy-done.2
  21.9 0.0 copy-start.8
  21.9 1.9 %gather_fusion.1 = bf16[224,1024]{1,0:T(8,128)(2,1)} fusion(bf16[224,1024]{1,0:T(8,128)(2,1)S(1)} %copy-done.2, s32[1024]{0:T(1024)S(1)} %pad_clamp_fusion), kind=kCustom, calls=%fused_computation.1 | custom fusion | bytes 918400 | tf_op jit(solution)/shard_map/gather | solution.py:62
  23.8 0.0 copy-done.8
  23.8 0.1 broadcast_compare_fusion
  23.9 0.8 copy.81
  24.7 5.3 %all-to-all-done = bf16[4,56,1024]{2,1,0:T(8,128)(2,1)S(1)} async-done(((bf16[4,56,1024]{2,1,0:T(8,128)(2,1)}), bf16[4,56,1024]{2,1,0:T(8,128)(2,1)S(1)}, u32[]{:S(2)}, u32[]{:S(2)}) %all-to-all-start) | async-done | bytes 458784 | tf_op jit(solution)/shard_map/all_to_all | solution.py:66
  30.0 3.5 %all-to-all-start.1 = ((bf16[4,56,1024]{2,1,0:T(8,128)(2,1)}), bf16[4,56,1024]{2,1,0:T(8,128)(2,1)S(1)}, u32[]{:S(2)}, u32[]{:S(2)}) async-start(bf16[4,56,1024]{2,1,0:T(8,128)(2,1)} %bitcast.3), calls=%async_computation.1 | async-start | bytes 917504 | tf_op jit(solution)/shard_map/all_to_all | solution.py:67
  33.5 0.1 copy.79
  33.6 0.0 copy-start.6
  33.6 0.0 copy-start.7
  33.6 0.3 multiply_reduce_fusion.5
  33.9 0.1 copy.59
  34.0 7.6 %all-to-all-done.1 = bf16[4,56,1024]{2,1,0:T(8,128)(2,1)S(1)} async-done(((bf16[4,56,1024]{2,1,0:T(8,128)(2,1)}), bf16[4,56,1024]{2,1,0:T(8,128)(2,1)S(1)}, u32[]{:S(2)}, u32[]{:S(2)}) %all-to-all-start.1) | async-done | bytes 458784 | tf_op jit(solution)/shard_map/all_to_all | solution.py:67
  41.6 0.1 copy.80
  41.7 0.3 multiply_reduce_fusion.4
  42.0 0.1 copy.60
  42.1 0.0 copy-done.6
  42.1 0.0 copy-done.7
  42.1 0.5 multiply_convert_fusion.2
  42.6 0.0 copy-start.3
  42.6 2.0 %fusion.27 = (f32[8,224]{1,0:T(8,128)S(1)}, f32[8,224,224]{1,2,0:T(8,128)}) fusion(pred[224,224]{0,1:T(8,128)(4,1)S(1)} %broadcast_compare_fusion, bf16[224,8,128]{2,0,1:T(8,128)(2,1)S(1)} %get-tuple-element.15, bf16[224,8,128]{2,0,1:T(8,128)(2,1)S(1)} %get-tuple-element.16), kind=kOutput, calls=%fused_computation.59 | convolution fusion | flops 104366304 | bytes 2580480 | tf_op jit(solution)/shard_map/sub | solution.py:35
  44.6 0.0 copy-done.3
  44.6 0.0 copy-done
  44.7 2.0 %fusion.6 = bf16[8,28,8,128]{3,2,1,0:T(8,128)(2,1)S(1)} fusion(f32[8,224,224]{1,2,0:T(8,128)} %get-tuple-element.12, f32[8,224]{1,0:T(8,128)S(1)} %get-tuple-element.11, bf16[224,1024]{1,0:T(8,128)(2,1)S(1)} %copy-done), kind=kOutput, calls=%fused_computation.17 | convolution fusion | flops 103792640 | bytes 2530304 | tf_op jit(solution)/shard_map/hts,thd->shd/dot_general | solution.py:42
  46.7 0.0 copy-done.5
  46.7 0.1 copy-done.9
  46.9 0.6 fusion.5
  47.5 0.5 fusion.2
  48.0 0.0 copy-start.4
  48.1 1.5 %multiply_reduce_fusion = (f32[128]{0:T(128)S(1)}, f32[224,8]{0,1:T(8,128)S(1)}, f32[224,8,128]{2,0,1:T(8,128)}) fusion(f32[224,8,128]{2,1,0:T(8,128)S(1)} %bitcast.79, f32[224,8]{0,1:T(8,128)S(1)} %add_rsqrt_fusion, f32[128]{0:T(128)S(1)} %copy-done.6, bf16[8,224,224]{1,2,0:T(8,128)(2,1)S(1)} %fusion.2, bf16[224,8,128]{2,0,1:T(8,128)(2,1)S(1)} %get-tuple-element.15), kind=kOutput, calls=%fused_computation.20 | convolution fusion | flops 104134784 | bytes 3111936 | tf_op jit(solution)/shard_map/hts,thd->shd/dot_general | solution.py:49
  49.5 0.0 copy-done.4
  49.5 1.0 %multiply_reduce_fusion.1 = (f32[128]{0:T(128)S(1)}, f32[224,8]{0,1:T(8,128)S(1)}, f32[224,8,128]{2,0,1:T(8,128)S(1)}) fusion(f32[224,8,128]{2,1,0:T(8,128)S(1)} %bitcast.75, f32[224,8]{0,1:T(8,128)S(1)} %add_rsqrt_fusion.1, f32[128]{0:T(128)S(1)} %copy-done.7, bf16[224,8,128]{2,0,1:T(8,128)(2,1)S(1)} %copy-done.4, bf16[8,224,224]{1,2,0:T(8,128)(2,1)S(1)} %fusion.2), kind=kOutput, calls=%fused_computation.21 | convolution fusion | flops 104134784 | bytes 3111936 | tf_op jit(solution)/shard_map/hts,shd->thd/dot_general | solution.py:48
  50.5 0.9 copy.122
  51.4 40.2 %all-reduce = (f32[128]{0:T(128)}, f32[128]{0:T(128)}) all-reduce(f32[128]{0:T(128)S(1)} %get-tuple-element.7, f32[128]{0:T(128)S(1)} %get-tuple-element.5), channel_id=1, replica_groups=mesh['dp'=4,'fsdp'=8] {'dp','fsdp'}, use_global_device_ids=true, to_apply=%region_9.10 | all-reduce | flops 256 | bytes 2048 | tf_op jit(solution)/shard_map/psum | solution.py:73
  91.6 2.5 %copy_bitcast_fusion.1 = bf16[224,1024]{1,0:T(8,128)(2,1)} fusion(f32[224,8,128]{2,1,0:T(8,128)S(1)} %bitcast.80, f32[224,8,128]{2,0,1:T(8,128)} %get-tuple-element.14, f32[224,8]{0,1:T(8,128)S(1)} %broadcast_multiply_fusion, f32[128]{0:T(128)S(1)} %copy-done.6, f32[224,8]{0,1:T(8,128)S(1)} %add_rsqrt_fusion), kind=kLoop, calls=%fused_computation.38 | loop fusion | flops 1376256 | bytes 2308608 | tf_op jit(solution)/shard_map/convert_element_type | solution.py:21
  94.1 1.3 %copy_bitcast_fusion.2 = bf16[224,1024]{1,0:T(8,128)(2,1)} fusion(f32[224,8,128]{2,1,0:T(8,128)S(1)} %bitcast.76, f32[224,8,128]{2,0,1:T(8,128)S(1)} %get-tuple-element.13, f32[224,8]{0,1:T(8,128)S(1)} %broadcast_multiply_fusion.1, f32[128]{0:T(128)S(1)} %copy-done.7, f32[224,8]{0,1:T(8,128)S(1)} %add_rsqrt_fusion.1), kind=kLoop, calls=%fused_computation.39 | loop fusion | flops 1376256 | bytes 2308608 | tf_op jit(solution)/shard_map/convert_element_type | solution.py:21
  (9 shorter events, 0.0 us)
Async XLA Ops:
  0.6 44.0 %copy-start = (bf16[224,1024]{1,0:T(8,128)(2,1)S(1)}, bf16[224,1024]{1,0:T(8,128)(2,1)}, u32[]{:S(2)}) copy-start(bf16[224,1024]{1,0:T(8,128)(2,1)} %param.13) | copy-start | bytes 1376260
  2.7 7.5 %copy-start.1 = (bf16[224,1024]{1,0:T(8,128)(2,1)S(1)}, bf16[224,1024]{1,0:T(8,128)(2,1)}, u32[]{:S(2)}) copy-start(bf16[224,1024]{1,0:T(8,128)(2,1)} %param.8) | copy-start | bytes 1376260
  6.1 12.4 %all-to-all-start.2 = ((bf16[4,56,1024]{2,1,0:T(8,128)(2,1)}), bf16[4,56,1024]{2,1,0:T(8,128)(2,1)S(1)}, u32[]{:S(2)}, u32[]{:S(2)}) async-start(bf16[4,56,1024]{2,1,0:T(8,128)(2,1)} %bitcast.5), calls=%async_computation.2 | async-start | bytes 917504 | tf_op jit(solution)/shard_map/all_to_all | solution.py:68
  10.3 11.6 %copy-start.2 = (bf16[224,1024]{1,0:T(8,128)(2,1)S(1)}, bf16[224,1024]{1,0:T(8,128)(2,1)}, u32[]{:S(2)}) copy-start(bf16[224,1024]{1,0:T(8,128)(2,1)} %param.9) | copy-start | bytes 1376260
  18.4 11.6 %all-to-all-start = ((bf16[4,56,1024]{2,1,0:T(8,128)(2,1)}), bf16[4,56,1024]{2,1,0:T(8,128)(2,1)S(1)}, u32[]{:S(2)}, u32[]{:S(2)}) async-start(bf16[4,56,1024]{2,1,0:T(8,128)(2,1)} %bitcast.2), calls=%async_computation | async-start | bytes 917504 | tf_op jit(solution)/shard_map/all_to_all | solution.py:66
  21.9 1.9 %copy-start.8 = (s32[1,224]{1,0:T(1,128)S(1)}, s32[1,224]{1,0:T(1,128)}, u32[]{:S(2)}) copy-start(s32[1,224]{1,0:T(1,128)} %param.12) | copy-start | bytes 2692
  30.0 11.6 %all-to-all-start.1 = ((bf16[4,56,1024]{2,1,0:T(8,128)(2,1)}), bf16[4,56,1024]{2,1,0:T(8,128)(2,1)S(1)}, u32[]{:S(2)}, u32[]{:S(2)}) async-start(bf16[4,56,1024]{2,1,0:T(8,128)(2,1)} %bitcast.3), calls=%async_computation.1 | async-start | bytes 917504 | tf_op jit(solution)/shard_map/all_to_all | solution.py:67
  33.6 8.5 %copy-start.6 = (f32[128]{0:T(128)S(1)}, f32[128]{0:T(128)}, u32[]{:S(2)}) copy-start(f32[128]{0:T(128)} %param.15) | copy-start | bytes 1540
  33.6 8.5 %copy-start.7 = (f32[128]{0:T(128)S(1)}, f32[128]{0:T(128)}, u32[]{:S(2)}) copy-start(f32[128]{0:T(128)} %param.14) | copy-start | bytes 1540
  42.6 2.0 %copy-start.3 = (bf16[224,8,128]{2,0,1:T(8,128)(2,1)}, bf16[224,8,128]{2,0,1:T(8,128)(2,1)S(1)}, u32[]{:S(2)}) copy-start(bf16[224,8,128]{2,0,1:T(8,128)(2,1)S(1)} %get-tuple-element.16) | copy-start | bytes 1376260
  44.6 2.1 %copy-start.5 = (bf16[28,8,8,128]{3,2,1,0:T(8,128)(2,1)S(1)}, bf16[28,8,8,128]{3,2,1,0:T(8,128)(2,1)}, u32[]{:S(2)}) copy-start(bf16[28,8,8,128]{3,2,1,0:T(8,128)(2,1)} %copy.81) | copy-start | bytes 1376260
  44.7 2.2 %copy-start.9 = (f32[8,224,224]{1,2,0:T(8,128)S(1)}, f32[8,224,224]{1,2,0:T(8,128)}, u32[]{:S(2)}) copy-start(f32[8,224,224]{1,2,0:T(8,128)} %get-tuple-element.12) | copy-start | bytes 4816900
  48.0 1.5 %copy-start.4 = (bf16[224,8,128]{2,0,1:T(8,128)(2,1)S(1)}, bf16[224,8,128]{2,0,1:T(8,128)(2,1)}, u32[]{:S(2)}) copy-start(bf16[224,8,128]{2,0,1:T(8,128)(2,1)} %copy-done.3) | copy-start | bytes 1376260
where the time goes:
time: 95.9 us; the launch traced here: 95.4 us
  blocking collectives  40.2 us (42%)
  waiting for transfers between devices  19.2 us (20%)
  starting transfers between devices  11.1 us (12%)
  local copies, waits for them, and re-layouts  10.6 us (11%)
  matrix products  7.69 us (8%)
  other arithmetic  5.83 us (6%)
    psum x1, blocking collectives, on_device(): query_total, key_total = lax.psum((query_part, key_part), ('dp', 'fsdp'))  40.2 us
    all_to_all x1, waiting for transfers between devices, on_device(): lax.all_to_all(send_key, 'dp', split_axis=0, concat_axis=0, tiled=True)  7.6 us
    all_to_all x1, waiting for transfers between devices, on_device(): lax.all_to_all(send_value, 'dp', split_axis=0, concat_axis=0, tiled=True)  6.28 us
    all_to_all x1, waiting for transfers between devices, on_device(): lax.all_to_all(send_query, 'dp', split_axis=0, concat_axis=0, tiled=True)  5.27 us
    all_to_all x1, starting transfers between devices, on_device(): lax.all_to_all(send_value, 'dp', split_axis=0, concat_axis=0, tiled=True)  4.21 us
    convert_element_type x2, other arithmetic, norm_back(): return result.reshape(result.shape[0], -1).astype(jnp.bfloat16)  3.8 us
    all_to_all x1, starting transfers between devices, on_device(): lax.all_to_all(send_query, 'dp', split_axis=0, concat_axis=0, tiled=True)  3.47 us
    all_to_all x1, starting transfers between devices, on_device(): lax.all_to_all(send_key, 'dp', split_axis=0, concat_axis=0, tiled=True)  3.47 us
  transfers between devices with their start and end apart: 3, of which 3 were waited for; matrix products, arithmetic and copies ran while one was open for 5% of the time, Pallas kernels for 0%

commit v1 on v0

v1 whole, which is shorter than its diff:
```python
import functools
import math

import jax
import jax.numpy as jnp
from jax import lax
from jax.experimental import pallas as pl
from jax.experimental.pallas import tpu as pltpu
from jax.sharding import PartitionSpec as P

HEAD = 128
PER = 2
MESH = pl.DeviceIdType.MESH
F32, BF16 = jnp.float32, jnp.bfloat16


def mm(a, b, contract):
    return lax.dot_general(a, b, ((contract[:1], contract[1:]), ((), ())), preferred_element_type=F32)


def kernel(
    n_dp, n_fs,
    q_hbm, k_hbm, v_hbm, plan_ref, seg_ref, g_hbm, qgain_ref, kgain_ref,
    qgrad_ref, kgrad_ref, vgrad_ref, qsum_ref, ksum_ref,
    q_in, k_in, v_in, g_in, send, recv, onehot, bias, acc, red_dp, red_fs,
    in_sem, send_sem, recv_sem, dp_send, dp_recv, fs_send, fs_recv,
):
    frames = q_in.shape[0]
    rows = frames // n_dp
    chunks, _, height, _ = send.shape
    padded = height // (3 * PER)
    width = PER * HEAD
    me = lax.axis_index("dp")
    mf = lax.axis_index("fsdp")

    loads = [
        pltpu.make_async_copy(src, dst, in_sem.at[i])
        for i, (src, dst) in enumerate(((q_hbm, q_in), (k_hbm, k_in), (v_hbm, v_in), (g_hbm, g_in)))
    ]
    for load in loads:
        load.start()
    barrier = pltpu.get_barrier_semaphore()
    for k in range(1, n_dp):
        pl.semaphore_signal(barrier, inc=1, device_id={"dp": lax.rem(me + k, n_dp)}, device_id_type=MESH)
    for k in range(1, n_fs):
        pl.semaphore_signal(barrier, inc=1, device_id={"fsdp": lax.rem(mf + k, n_fs)}, device_id_type=MESH)

    order = lax.broadcasted_iota(jnp.int32, (n_dp * padded, 1), 0)
    if padded != rows:
        within = order % padded
        order = jnp.where(within < rows, order // padded * rows + within, -1)
    onehot[...] = (order == plan_ref[...]).astype(F32).astype(BF16)
    for load in loads[:3]:
        load.wait()

    def hop(c, k):
        to = lax.rem(me + k, n_dp)
        return pltpu.make_async_remote_copy(
            src_ref=send.at[c, to], dst_ref=recv.at[c, me],
            send_sem=send_sem.at[c, k], recv_sem=recv_sem.at[c, k],
            device_id={"dp": to}, device_id_type=MESH,
        )

    def stay(c):
        return pltpu.make_async_copy(send.at[c, me], recv.at[c, me], recv_sem.at[c, 0])

    def gather(c):
        cols = pl.ds(pl.multiple_of(c * width, width), width)
        sorted_rows = [mm(onehot[...], ref[:, cols], (1, 0)) for ref in (q_in, k_in, v_in)]
        for d in range(n_dp):
            span = slice(d * padded, (d + 1) * padded)
            send[c, d] = jnp.concatenate(
                [x[span, i * HEAD:(i + 1) * HEAD] for i in range(PER) for x in sorted_rows], axis=0
            ).astype(BF16)

    def launch(c):
        for k in range(1, n_dp):
            hop(c, k).start()
        stay(c).start()

    gather(0)
    pl.semaphore_wait(barrier, n_dp - 1 + n_fs - 1)
    launch(0)

    @pl.loop(1, chunks)
    def _(c):
        gather(c)
        launch(c)

    seg_row = jnp.broadcast_to(seg_ref[...].astype(F32), (frames, frames))
    i0 = lax.broadcasted_iota(jnp.int32, (frames, frames), 0)
    i1 = lax.broadcasted_iota(jnp.int32, (frames, frames), 1)
    seg_col = jnp.sum(jnp.where(i0 == i1, seg_row, 0.0), axis=1, keepdims=True)
    bias[...] = jnp.where(seg_col == seg_row, 0.0, -jnp.inf)
    acc[...] = jnp.zeros_like(acc)
    loads[3].wait()

    scale = HEAD ** (-0.5)
    q_gain, k_gain = qgain_ref[...], kgain_ref[...]

    @pl.loop(0, chunks)
    def _(c):
        stay(c).wait()
        for k in range(1, n_dp):
            came = lax.rem(me + n_dp - k, n_dp)
            pltpu.make_async_remote_copy(
                src_ref=send.at[c, came], dst_ref=recv.at[c, came],
                send_sem=send_sem.at[c, k], recv_sem=recv_sem.at[c, k],
                device_id={"dp": came}, device_id_type=MESH,
            ).wait_recv()
        blocks = [recv[c, s].astype(F32) for s in range(n_dp)]
        for i in range(PER):
            cols = pl.ds(pl.multiple_of(c * width + i * HEAD, HEAD), HEAD)

            def packed(a):
                at = (3 * i + a) * padded
                return jnp.concatenate([b[at:at + rows] for b in blocks], axis=0)

            q, k, v = packed(0), packed(1), packed(2).astype(BF16)
            g = g_in[:, cols]
            q_inv = lax.rsqrt(jnp.mean(q * q, axis=-1, keepdims=True) + 1e-06)
            k_inv = lax.rsqrt(jnp.mean(k * k, axis=-1, keepdims=True) + 1e-06)
            q_unit, k_unit = q * q_inv, k * k_inv
            q_norm, k_norm = (q_unit * q_gain).astype(BF16), (k_unit * k_gain).astype(BF16)
            scores = mm(k_norm, q_norm, (1, 1)) + bias[...]
            top = jnp.max(scores, axis=0, keepdims=True)
            e = jnp.exp2((scores - top) * (scale * math.log2(math.e)))
            probs = e * (1.0 / jnp.sum(e, axis=0, keepdims=True))
            half = probs.astype(BF16)
            d_prob = mm(v, g, (1, 1))
            delta = jnp.sum(half.astype(F32) * d_prob, axis=0, keepdims=True)
            d_score = (probs * (d_prob - delta) * scale).astype(BF16)
            vgrad_ref[:, cols] = mm(half, g, (1, 0)).astype(BF16)
            d_k = mm(d_score, q_norm, (1, 0))
            d_q = mm(d_score, k_norm, (0, 0))
            for out, at, d_norm, unit, inv, gain in (
                (qgrad_ref, 0, d_q, q_unit, q_inv, q_gain),
                (kgrad_ref, 1, d_k, k_unit, k_inv, k_gain),
            ):
                both = d_norm * unit
                acc[at] += jnp.sum(both.reshape(frames // 8, 8, HEAD), axis=0)
                inner = jnp.mean(both * gain, axis=-1, keepdims=True)
                out[:, cols] = (inv * (d_norm * gain - unit * inner)).astype(BF16)

    def exchange(axis, n, mine, slots, ssem, rsem):
        copies = []
        for k in range(1, n):
            copy = pltpu.make_async_remote_copy(
                src_ref=slots.at[mine], dst_ref=slots.at[mine],
                send_sem=ssem.at[k], recv_sem=rsem.at[k],
                device_id={axis: lax.rem(mine + k, n)}, device_id_type=MESH,
            )
            copy.start()
            copies.append(copy)
        for k in range(1, n):
            came = lax.rem(mine + n - k, n)
            pltpu.make_async_remote_copy(
                src_ref=slots.at[came], dst_ref=slots.at[came],
                send_sem=ssem.at[k], recv_sem=rsem.at[k],
                device_id={axis: came}, device_id_type=MESH,
            ).wait_recv()
        return copies

    red_dp[me] = jnp.sum(acc[...], axis=1)
    sent = exchange("dp", n_dp, me, red_dp, dp_send, dp_recv)
    total = red_dp[0]
    for s in range(1, n_dp):
        total = total + red_dp[s]
    red_fs[mf] = total
    sent += exchange("fsdp", n_fs, mf, red_fs, fs_send, fs_recv)
    total = red_fs[0]
    for s in range(1, n_fs):
        total = total + red_fs[s]
    qsum_ref[...] = total[0:1]
    ksum_ref[...] = total[1:2]
    for copy in sent:
        copy.wait_send()

    @pl.loop(0, chunks)
    def _(c):
        for k in range(1, n_dp):
            hop(c, k).wait_send()


def on_device(n_dp, n_fs, query_in, key_in, value_in, length_plan, segment_ids, out_grad, query_gain, key_gain):
    frames, hid = query_in.shape
    rows = frames // n_dp
    padded = -(-rows // 8) * 8
    chunks = hid // (PER * HEAD)
    vmem = pl.BlockSpec(memory_space=pltpu.VMEM)
    hbm = pl.BlockSpec(memory_space=pl.ANY)
    wide = jax.ShapeDtypeStruct((frames, hid), BF16)
    line = jax.ShapeDtypeStruct((1, HEAD), F32)
    dma = pltpu.SemaphoreType.DMA
    outs = pl.pallas_call(
        functools.partial(kernel, n_dp, n_fs),
        out_shape=(wide, wide, wide, line, line),
        in_specs=[hbm, hbm, hbm, vmem, vmem, hbm, vmem, vmem],
        out_specs=(vmem,) * 5,
        scratch_shapes=[
            pltpu.VMEM((frames, hid), BF16),
            pltpu.VMEM((frames, hid), BF16),
            pltpu.VMEM((frames, hid), BF16),
            pltpu.VMEM((frames, hid), BF16),
            pltpu.VMEM((chunks, n_dp, 3 * PER * padded, HEAD), BF16),
            pltpu.VMEM((chunks, n_dp, 3 * PER * padded, HEAD), BF16),
            pltpu.VMEM((n_dp * padded, frames), BF16),
            pltpu.VMEM((frames, frames), F32),
            pltpu.VMEM((2, 8, HEAD), F32),
            pltpu.VMEM((n_dp, 2, HEAD), F32),
            pltpu.VMEM((n_fs, 2, HEAD), F32),
            dma((4,)),
            dma((chunks, n_dp)),
            dma((chunks, n_dp)),
            dma((n_dp,)),
            dma((n_dp,)),
            dma((n_fs,)),
            dma((n_fs,)),
        ],
        compiler_params=pltpu.CompilerParams(
            collective_id=0, has_side_effects=True, vmem_limit_bytes=32 * 1024 * 1024
        ),
    )(
        query_in, key_in, value_in, length_plan, segment_ids, out_grad,
        query_gain.reshape(1, HEAD), key_gain.reshape(1, HEAD),
    )
    q_grad, k_grad, v_grad, q_sum, k_sum = outs
    return (q_grad, k_grad, v_grad, q_sum.reshape(HEAD), k_sum.reshape(HEAD))


def solution(mesh):
    split = P(("dp", "fsdp"), None)
    return jax.shard_map(
        functools.partial(on_device, mesh.shape["dp"], mesh.shape["fsdp"]),
        mesh=mesh,
        in_specs=(split,) * 6 + (P(), P()),
        out_specs=(split,) * 3 + (P(), P()),
        check_vma=False,
    )
```

time: 95.9 us -> 39.4 us (0.41)
  blocking collectives: 40.2 us -> 0 us
  Pallas kernels: 0 us -> 30.3 us
  waiting for transfers between devices: 19.2 us -> 0 us
  starting transfers between devices: 11.1 us -> 0 us
  matrix products: 7.69 us -> 0 us
  other arithmetic: 5.83 us -> 0 us
  local copies, waits for them, and re-layouts: 10.6 us -> 8.08 us
    psum x1 -> x0, blocking collectives: 40.2 us -> none  [on_device(): query_total, key_total = lax.psum((query_part, key_part), ('dp', 'fsdp'))]
    pallas_call x0 -> x1, Pallas kernels: none -> 30.3 us  [on_device(): pl.pallas_call(functools.partial(kernel, n_dp, n_fs), out_shape=(wide, wi...]
    all_to_all x3 -> x0, waiting for transfers between devices: 19.2 us -> none  [the longest x1 7.6 us: on_device(): lax.all_to_all(send_key, 'dp', split_axis=0, concat_axis=0, tiled=True)]
    all_to_all x3 -> x0, starting transfers between devices: 11.1 us -> none  [the longest x1 4.21 us: on_device(): lax.all_to_all(send_value, 'dp', split_axis=0, concat_axis=0, tiled=True)]
    gather x3 -> x0, local copies, waits for them, and re-layouts: 7.05 us -> none  [the longest x1 3.33 us: on_device(): send_value = value_in[inverse]]
    unnamed x23 -> x21, local copies, waits for them, and re-layouts: 1.22 us -> 8.08 us
    dot_general x5 -> x0, matrix products: 5.69 us -> none  [the longest x1 2.05 us: attend_heads(): jnp.einsum('hts,thd->shd', probs_half, grad_heads, preferred_element_type...]
    convert_element_type x3 -> x0, other arithmetic: 4.34 us -> none  [the longest x2 3.8 us: norm_back(): return result.reshape(result.shape[0], -1).astype(jnp.bfloat16)]
  transfers between devices with their start and end apart: 3 -> 0, of which waited for: 3 -> 0; matrix products, arithmetic and copies ran while one was open for 5% -> 0% of each run, Pallas kernels for 0% -> 0%
where the time goes in v1:
time: 39.4 us; the launch traced here: 39.1 us
  Pallas kernels  30.3 us (77%)
  local copies, waits for them, and re-layouts  8.08 us (21%)
  between operations  0.68 us (2%)
    pallas_call x1, Pallas kernels, on_device(): pl.pallas_call(functools.partial(kernel, n_dp, n_fs), out_shape=(wide, wi...  30.3 us
    unnamed x21, local copies, waits for them, and re-layouts  8.08 us

profile of v1, /device:TPU:0, one launch (start us, length us, event | category | flops | bytes accessed | tf_op | source)
XLA Modules:
  0.0 39.1 jit_solution(8541087271295118568)
XLA Ops:
  0.6 0.0 copy-start.5
  0.6 0.0 copy-start.7
  0.7 0.0 copy-start.4
  0.7 0.0 copy-start.6
  0.7 0.6 %copy-done.5 = s32[1,224]{1,0:T(1,128)S(1)} copy-done((s32[1,224]{1,0:T(1,128)S(1)}, s32[1,224]{1,0:T(1,128)}, u32[]{:S(2)}) %copy-start.5) | copy-done | bytes 920
  1.3 0.0 copy-done.7
  1.3 0.0 copy-done.4
  1.3 0.0 copy-done.6
  1.3 0.0 copy-start
  1.4 1.0 %copy-done = bf16[224,1024]{1,0:T(8,128)(2,1)S(1)} copy-done((bf16[224,1024]{1,0:T(8,128)(2,1)S(1)}, bf16[224,1024]{1,0:T(8,128)(2,1)}, u32[]{:S(2)}) %copy-start) | copy-done | bytes 458776
  2.4 0.0 copy-start.1
  2.4 1.0 %copy-done.1 = bf16[224,1024]{1,0:T(8,128)(2,1)S(1)} copy-done((bf16[224,1024]{1,0:T(8,128)(2,1)S(1)}, bf16[224,1024]{1,0:T(8,128)(2,1)}, u32[]{:S(2)}) %copy-start.1) | copy-done | bytes 458776
  3.4 0.0 copy-start.2
  3.4 1.0 %copy-done.2 = bf16[224,1024]{1,0:T(8,128)(2,1)S(1)} copy-done((bf16[224,1024]{1,0:T(8,128)(2,1)S(1)}, bf16[224,1024]{1,0:T(8,128)(2,1)}, u32[]{:S(2)}) %copy-start.2) | copy-done | bytes 458776
  4.4 0.0 copy-start.3
  4.4 1.0 %copy-done.3 = bf16[224,1024]{1,0:T(8,128)(2,1)S(1)} copy-done((bf16[224,1024]{1,0:T(8,128)(2,1)S(1)}, bf16[224,1024]{1,0:T(8,128)(2,1)}, u32[]{:S(2)}) %copy-start.3) | copy-done | bytes 458776
  5.4 30.3 %shard_map.119 = (bf16[224,1024]{1,0:T(8,128)(2,1)S(1)}, bf16[224,1024]{1,0:T(8,128)(2,1)S(1)}, bf16[224,1024]{1,0:T(8,128)(2,1)S(1)}, f32[1,128]{1,0:T(1,128)S(1)}, f32[1,128]{1,0:T(1,128)S(1)}) custom-call(bf16[224,1024]{1,0:T(8,128)(2,1)S(1)} %copy-done, bf16[224,1024]{1,0:T(8,128)(2,1)S(1)} %copy-done.1, bf16[224,1024]{1,0:T(8,128)(2,1)S(1)} %copy-done.2, ...), custom_call_target="tpu_custom_call" | custom-call | tf_op jit(solution)/shard_map/pallas_call | solution.py:195
  35.7 0.8 %copy.18 = bf16[224,1024]{1,0:T(8,128)(2,1)} copy(bf16[224,1024]{1,0:T(8,128)(2,1)S(1)} %get-tuple-element.20) | data formatting | bytes 917504
  36.5 0.8 %copy.19 = bf16[224,1024]{1,0:T(8,128)(2,1)} copy(bf16[224,1024]{1,0:T(8,128)(2,1)S(1)} %get-tuple-element.21) | data formatting | bytes 917504
  37.3 0.8 %copy.20 = bf16[224,1024]{1,0:T(8,128)(2,1)} copy(bf16[224,1024]{1,0:T(8,128)(2,1)S(1)} %get-tuple-element.22) | data formatting | bytes 917504
  38.0 0.5 %copy.21 = f32[128]{0:T(128)} copy(f32[128]{0:T(128)S(1)} %bitcast.7) | data formatting | bytes 1024
  38.5 0.5 %copy.22 = f32[128]{0:T(128)} copy(f32[128]{0:T(128)S(1)} %bitcast.6) | data formatting | bytes 1024
Async XLA Ops:
  0.6 0.7 %copy-start.5 = (s32[1,224]{1,0:T(1,128)S(1)}, s32[1,224]{1,0:T(1,128)}, u32[]{:S(2)}) copy-start(s32[1,224]{1,0:T(1,128)} %seg_ref.1) | copy-start | bytes 2692
  0.6 0.7 %copy-start.7 = (f32[128]{0:T(128)S(1)}, f32[128]{0:T(128)}, u32[]{:S(2)}) copy-start(f32[128]{0:T(128)} %param.15) | copy-start | bytes 1540
  0.7 0.7 %copy-start.4 = (s32[1,224]{1,0:T(1,128)S(1)}, s32[1,224]{1,0:T(1,128)}, u32[]{:S(2)}) copy-start(s32[1,224]{1,0:T(1,128)} %plan_ref.1) | copy-start | bytes 2692
  0.7 0.7 %copy-start.6 = (f32[128]{0:T(128)S(1)}, f32[128]{0:T(128)}, u32[]{:S(2)}) copy-start(f32[128]{0:T(128)} %param.14) | copy-start | bytes 1540
  1.3 1.0 %copy-start = (bf16[224,1024]{1,0:T(8,128)(2,1)S(1)}, bf16[224,1024]{1,0:T(8,128)(2,1)}, u32[]{:S(2)}) copy-start(bf16[224,1024]{1,0:T(8,128)(2,1)} %q_hbm.1) | copy-start | bytes 1376260
  2.4 1.0 %copy-start.1 = (bf16[224,1024]{1,0:T(8,128)(2,1)S(1)}, bf16[224,1024]{1,0:T(8,128)(2,1)}, u32[]{:S(2)}) copy-start(bf16[224,1024]{1,0:T(8,128)(2,1)} %k_hbm.1) | copy-start | bytes 1376260
  3.4 1.0 %copy-start.2 = (bf16[224,1024]{1,0:T(8,128)(2,1)S(1)}, bf16[224,1024]{1,0:T(8,128)(2,1)}, u32[]{:S(2)}) copy-start(bf16[224,1024]{1,0:T(8,128)(2,1)} %v_hbm.1) | copy-start | bytes 1376260
  4.4 1.0 %copy-start.3 = (bf16[224,1024]{1,0:T(8,128)(2,1)S(1)}, bf16[224,1024]{1,0:T(8,128)(2,1)}, u32[]{:S(2)}) copy-start(bf16[224,1024]{1,0:T(8,128)(2,1)} %g_hbm.1) | copy-start | bytes 1376260

commit v2 on v1

--- a/solution.py
+++ b/solution.py
@@ -10,6 +10,8 @@
 
 HEAD = 128
 PER = 2
+AHEAD = 2
+GRANT = 60 * 1024 * 1024
 MESH = pl.DeviceIdType.MESH
 F32, BF16 = jnp.float32, jnp.bfloat16
 
@@ -20,10 +22,12 @@
 
 def kernel(
     n_dp, n_fs,
-    q_hbm, k_hbm, v_hbm, plan_ref, seg_ref, g_hbm, qgain_ref, kgain_ref,
-    qgrad_ref, kgrad_ref, vgrad_ref, qsum_ref, ksum_ref,
-    q_in, k_in, v_in, g_in, send, recv, onehot, bias, acc, red_dp, red_fs,
-    in_sem, send_sem, recv_sem, dp_send, dp_recv, fs_send, fs_recv,
+    q_hbm, k_hbm, v_hbm, plan_hbm, seg_hbm, g_hbm, qgain_hbm, kgain_hbm,
+    qgrad_hbm, kgrad_hbm, vgrad_hbm, qsum_ref, ksum_ref,
+    qgrad_ref, kgrad_ref, vgrad_ref, out_sem,
+    q_in, k_in, v_in, g_in, plan_ref, seg_ref, qgain_ref, kgain_ref,
+    send, recv, onehot, bias, acc, red_dp, red_fs,
+    in_sem, small_sem, send_sem, recv_sem, dp_send, dp_recv, fs_send, fs_recv,
 ):
     frames = q_in.shape[0]
     rows = frames // n_dp
@@ -33,12 +37,24 @@
     me = lax.axis_index("dp")
     mf = lax.axis_index("fsdp")
 
-    loads = [
-        pltpu.make_async_copy(src, dst, in_sem.at[i])
-        for i, (src, dst) in enumerate(((q_hbm, q_in), (k_hbm, k_in), (v_hbm, v_in), (g_hbm, g_in)))
+    def load(i, c):
+        src, dst = ((q_hbm, q_in), (k_hbm, k_in), (v_hbm, v_in), (g_hbm, g_in))[i]
+        cols = pl.ds(pl.multiple_of(c * width, width), width)
+        return pltpu.make_async_copy(src.at[:, cols], dst.at[:, cols], in_sem.at[i, c])
+
+    small = [
+        pltpu.make_async_copy(src, dst, small_sem.at[i])
+        for i, (src, dst) in enumerate(
+            ((plan_hbm, plan_ref), (seg_hbm, seg_ref), (qgain_hbm, qgain_ref), (kgain_hbm, kgain_ref))
+        )
     ]
-    for load in loads:
-        load.start()
+    for copy in small:
+        copy.start()
+    for c in range(chunks):
+        for i in range(3):
+            load(i, c).start()
+    for c in range(chunks):
+        load(3, c).start()
     barrier = pltpu.get_barrier_semaphore()
     for k in range(1, n_dp):
         pl.semaphore_signal(barrier, inc=1, device_id={"dp": lax.rem(me + k, n_dp)}, device_id_type=MESH)
@@ -49,9 +65,13 @@
     if padded != rows:
         within = order % padded
         order = jnp.where(within < rows, order // padded * rows + within, -1)
+    small[0].wait()
     onehot[...] = (order == plan_ref[...]).astype(F32).astype(BF16)
-    for load in loads[:3]:
-        load.wait()
+
+    def store(i, c):
+        src, dst = ((qgrad_ref, qgrad_hbm), (kgrad_ref, kgrad_hbm), (vgrad_ref, vgrad_hbm))[i]
+        cols = pl.ds(pl.multiple_of(c * width, width), width)
+        return pltpu.make_async_copy(src.at[:, cols], dst.at[:, cols], out_sem.at[i, c])
 
     def hop(c, k):
         to = lax.rem(me + k, n_dp)
@@ -65,6 +85,8 @@
         return pltpu.make_async_copy(send.at[c, me], recv.at[c, me], recv_sem.at[c, 0])
 
     def gather(c):
+        for i in range(3):
+            load(i, c).wait()
         cols = pl.ds(pl.multiple_of(c * width, width), width)
         sorted_rows = [mm(onehot[...], ref[:, cols], (1, 0)) for ref in (q_in, k_in, v_in)]
         for d in range(n_dp):
@@ -82,24 +104,37 @@
     pl.semaphore_wait(barrier, n_dp - 1 + n_fs - 1)
     launch(0)
 
-    @pl.loop(1, chunks)
+    for c in range(1, min(AHEAD, chunks)):
+        gather(c)
+        launch(c)
+
+    @pl.loop(min(AHEAD, chunks), chunks)
     def _(c):
         gather(c)
-        launch(c)
-
+
+    for copy in small[1:]:
+        copy.wait()
     seg_row = jnp.broadcast_to(seg_ref[...].astype(F32), (frames, frames))
     i0 = lax.broadcasted_iota(jnp.int32, (frames, frames), 0)
     i1 = lax.broadcasted_iota(jnp.int32, (frames, frames), 1)
     seg_col = jnp.sum(jnp.where(i0 == i1, seg_row, 0.0), axis=1, keepdims=True)
     bias[...] = jnp.where(seg_col == seg_row, 0.0, -jnp.inf)
     acc[...] = jnp.zeros_like(acc)
-    loads[3].wait()
+    for c in range(chunks):
+        load(3, c).wait()
 
     scale = HEAD ** (-0.5)
     q_gain, k_gain = qgain_ref[...], kgain_ref[...]
 
     @pl.loop(0, chunks)
     def _(c):
+        for k in range(1, n_dp):
+            hop(c, k).wait_send()
+
+        @pl.when(c + AHEAD < chunks)
+        def _():
+            launch(c + AHEAD)
+
         stay(c).wait()
         for k in range(1, n_dp):
             came = lax.rem(me + n_dp - k, n_dp)
@@ -142,6 +177,9 @@
                 inner = jnp.mean(both * gain, axis=-1, keepdims=True)
                 out[:, cols] = (inv * (d_norm * gain - unit * inner)).astype(BF16)
 
+        for i in range(3):
+            store(i, c).start()
+
     def exchange(axis, n, mine, slots, ssem, rsem):
         copies = []
         for k in range(1, n):
@@ -175,11 +213,19 @@
     ksum_ref[...] = total[1:2]
     for copy in sent:
         copy.wait_send()
-
-    @pl.loop(0, chunks)
-    def _(c):
-        for k in range(1, n_dp):
-            hop(c, k).wait_send()
+    for c in range(chunks):
+        for i in range(3):
+            store(i, c).wait()
+
+
+def deliver(*refs):
+    count = len(refs) // 2
+    sems = refs[-1]
+    copies = [pltpu.make_async_copy(refs[i], refs[count + i], sems.at[i]) for i in range(count)]
+    for copy in copies:
+        copy.start()
+    for copy in copies:
+        copy.wait()
 
 
 def on_device(n_dp, n_fs, query_in, key_in, value_in, length_plan, segment_ids, out_grad, query_gain, key_gain):
@@ -188,20 +234,29 @@
     padded = -(-rows // 8) * 8
     chunks = hid // (PER * HEAD)
     vmem = pl.BlockSpec(memory_space=pltpu.VMEM)
-    hbm = pl.BlockSpec(memory_space=pl.ANY)
+    hbm = pl.BlockSpec(memory_space=pltpu.HBM)
+    free = pl.BlockSpec(memory_space=pl.ANY)
     wide = jax.ShapeDtypeStruct((frames, hid), BF16)
     line = jax.ShapeDtypeStruct((1, HEAD), F32)
     dma = pltpu.SemaphoreType.DMA
     outs = pl.pallas_call(
         functools.partial(kernel, n_dp, n_fs),
         out_shape=(wide, wide, wide, line, line),
-        in_specs=[hbm, hbm, hbm, vmem, vmem, hbm, vmem, vmem],
-        out_specs=(vmem,) * 5,
+        in_specs=[hbm] * 8,
+        out_specs=(hbm, hbm, hbm, vmem, vmem),
         scratch_shapes=[
             pltpu.VMEM((frames, hid), BF16),
             pltpu.VMEM((frames, hid), BF16),
             pltpu.VMEM((frames, hid), BF16),
-            pltpu.VMEM((frames, hid), BF16),
+            dma((3, chunks)),
+            pltpu.VMEM((frames, hid), BF16),
+            pltpu.VMEM((frames, hid), BF16),
+            pltpu.VMEM((frames, hid), BF16),
+            pltpu.VMEM((frames, hid), BF16),
+            pltpu.VMEM((1, frames), jnp.int32),
+            pltpu.VMEM((1, frames), jnp.int32),
+            pltpu.VMEM((1, HEAD), F32),
+            pltpu.VMEM((1, HEAD), F32),
             pltpu.VMEM((chunks, n_dp, 3 * PER * padded, HEAD), BF16),
             pltpu.VMEM((chunks, n_dp, 3 * PER * padded, HEAD), BF16),
             pltpu.VMEM((n_dp * padded, frames), BF16),
@@ -209,6 +264,7 @@
             pltpu.VMEM((2, 8, HEAD), F32),
             pltpu.VMEM((n_dp, 2, HEAD), F32),
             pltpu.VMEM((n_fs, 2, HEAD), F32),
+            dma((4, chunks)),
             dma((4,)),
             dma((chunks, n_dp)),
             dma((chunks, n_dp)),
@@ -218,13 +274,20 @@
             dma((n_fs,)),
         ],
         compiler_params=pltpu.CompilerParams(
-            collective_id=0, has_side_effects=True, vmem_limit_bytes=32 * 1024 * 1024
+            collective_id=0, has_side_effects=True, vmem_limit_bytes=GRANT
         ),
     )(
         query_in, key_in, value_in, length_plan, segment_ids, out_grad,
         query_gain.reshape(1, HEAD), key_gain.reshape(1, HEAD),
     )
-    q_grad, k_grad, v_grad, q_sum, k_sum = outs
+    q_grad, k_grad, v_grad, q_sum, k_sum = pl.pallas_call(
+        deliver,
+        out_shape=(wide, wide, wide, line, line),
+        in_specs=[free] * 5,
+        out_specs=(hbm,) * 5,
+        scratch_shapes=[dma((5,))],
+        compiler_params=pltpu.CompilerParams(vmem_limit_bytes=GRANT),
+    )(*outs)
     return (q_grad, k_grad, v_grad, q_sum.reshape(HEAD), k_sum.reshape(HEAD))
 
 

time: 39.4 us -> 73.8 us (1.87)
  Pallas kernels: 30.3 us -> 73 us
  local copies, waits for them, and re-layouts: 8.08 us -> 0 us
    pallas_call x0 -> x1, Pallas kernels: none -> 42.9 us  [on_device(): pl.pallas_call(deliver, out_shape=(wide, wide, wide, line, line), in_spec...]
    unnamed x21 -> x0, local copies, waits for them, and re-layouts: 8.08 us -> none
where the time goes in v2:
time: 73.8 us; the launch traced here: 73.6 us
  Pallas kernels  73 us (99%)
    pallas_call x1, Pallas kernels, on_device(): pl.pallas_call(deliver, out_shape=(wide, wide, wide, line, line), in_spec...  42.9 us
    pallas_call x1, Pallas kernels, on_device(): pl.pallas_call(functools.partial(kernel, n_dp, n_fs), out_shape=(wide, wi...  30.1 us

profile of v2, /device:TPU:0, one launch (start us, length us, event | category | flops | bytes accessed | tf_op | source)
XLA Modules:
  0.0 73.6 jit_solution(5476332027030174797)
XLA Ops:
  0.6 30.1 %shard_map.119 = (bf16[224,1024]{1,0:T(8,128)(2,1)}, bf16[224,1024]{1,0:T(8,128)(2,1)}, bf16[224,1024]{1,0:T(8,128)(2,1)}, f32[1,128]{1,0:T(1,128)}, f32[1,128]{1,0:T(1,128)}) custom-call(bf16[224,1024]{1,0:T(8,128)(2,1)} %q_hbm.1, bf16[224,1024]{1,0:T(8,128)(2,1)} %k_hbm.1, bf16[224,1024]{1,0:T(8,128)(2,1)} %v_hbm.1, s32[1,224]{1,0:T(1,128)} %plan_hbm.1, ...), custom_call_target="tpu_custom_call" | custom-call | tf_op jit(solution)/shard_map/pallas_call | solution.py:242
  30.7 42.9 %shard_map.120 = (bf16[224,1024]{1,0:T(8,128)(2,1)}, bf16[224,1024]{1,0:T(8,128)(2,1)}, bf16[224,1024]{1,0:T(8,128)(2,1)}, f32[1,128]{1,0:T(1,128)}, f32[1,128]{1,0:T(1,128)}) custom-call(bf16[224,1024]{1,0:T(8,128)(2,1)} %get-tuple-element.15.refs_0_, bf16[224,1024]{1,0:T(8,128)(2,1)} %get-tuple-element.16.refs_1_, ...), custom_call_target="tpu_custom_call" | custom-call | tf_op jit(solution)/shard_map/pallas_call | solution.py:283
